TPU v7x, 32 devices: a whole 2x2x4 slice. The times are simulated.
32 devices in a mesh: groups: 2 (over x), wide: 16 (over z, y, core).
Axes of the slice: x: 2, y: 2, z: 4, core: 2. Of those that a mesh axis runs over, the one named last changes fastest.
Arguments:
- tokens: bfloat16 [512, 16384], P(('groups', 'wide')), parts along dimension 0, may hold values from -6 to 6
- base_weight: bfloat16 [16384, 16384], P(None, 'wide'), may hold values from -0.046875 to 0.046875
- shrink_blocks: bfloat16 [128, 16, 16384], P('wide'), may hold values from -0.046875 to 0.046875
- expand_blocks: bfloat16 [128, 16, 16384], P('wide'), may hold values from -1.5 to 1.5
- adapter_slot: int32 [128], replicated, may hold values from 0 to 127, each once
- seg_adapter: int32 [32, 4], P(('groups', 'wide')), parts along dimension 0, may hold values from 0 to 127
- seg_lengths: int32 [32, 4], P(('groups', 'wide')), parts along dimension 0, may hold values from 1 to 4, 12 in all within a row
Outputs:
- queries: bfloat16 [512, 16384], P(('groups', 'wide')), parts along dimension 0
There are 2 independent parts, one for each index of `groups`. A program takes and returns all parts, laid end to end along the dimension named above; an argument that names none is the same for every part. Nothing has to cross between parts.
Inputs may be any that keep to these rules, and one draw needn't show every extreme that they name: Adapter i's blocks stand at index adapter_slot[i] of shrink_blocks and expand_blocks; each slot is used once. `seg_lengths`: the 4 lengths of one index of wide sum to 12.
All inputs are finite; a program needn't handle non-finite values.
Results may differ from a plain program's by a relative error of at most 0.0048.
Values may be sent and summed in bfloat16 or wider, within the bound.
A program may use at most 128 MiB of HBM per device.

v0:
```python
import jax
import jax.numpy as jnp
from jax import lax
from jax.sharding import PartitionSpec as P


def rank_table(owned, capacity):
    order = jnp.cumsum(owned.astype(jnp.int32), axis=1) - 1
    levels = jnp.arange(capacity, dtype=jnp.int32)
    table = owned[:, None, :] & (order[:, None, :] == levels[None, :, None])
    return table.astype(jnp.bfloat16)


def body(tokens, base_weight, shrink_blocks, expand_blocks, adapter_slot, seg_adapter, seg_lengths):
    ids_all, lengths_all = (
        lax.all_gather(seg_adapter, "wide", axis=0, tiled=True),
        lax.all_gather(seg_lengths, "wide", axis=0, tiled=True),
    )
    segment_cap = tokens.shape[0] // seg_adapter.shape[1]
    local_count = shrink_blocks.shape[0]
    rank_size = shrink_blocks.shape[1]
    shrink_local_blocks = shrink_blocks.reshape(local_count * rank_size, -1)
    expand_local_blocks = expand_blocks.reshape(local_count * rank_size, -1)
    row_adapter = jnp.repeat(ids_all.reshape(-1), segment_cap)
    row_length = jnp.repeat(lengths_all.reshape(-1), segment_cap)
    position = jnp.arange(row_adapter.shape[0], dtype=jnp.int32) % segment_cap
    filled = position < row_length
    row_slot = jnp.take(adapter_slot, row_adapter)
    here = lax.axis_index("wide")
    column_slot = (
        here * local_count + jnp.arange(local_count * rank_size, dtype=jnp.int32) // rank_size
    )
    selected = filled[:, None] & (row_slot[:, None] == column_slot[None, :])
    out_columns = base_weight.shape[1]
    block_rows = lax.all_gather(tokens, "wide", axis=0, tiled=True)
    base_piece = jnp.dot(block_rows, base_weight, preferred_element_type=jnp.float32)
    shrink_piece = lax.dot_general(
        block_rows,
        shrink_local_blocks,
        (((1,), (1,)), ((), ())),
        preferred_element_type=jnp.float32,
    )
    joined = jnp.concatenate([base_piece, shrink_piece], axis=1)
    base_cols = joined[:, :out_columns]
    shrink_local = jnp.where(selected, joined[:, out_columns:], jnp.float32(0.0)).astype(
        jnp.bfloat16
    )
    peers = lax.axis_size("wide")
    my_rows = tokens.shape[0]
    capacity = 3 * seg_adapter.shape[1]
    slot_grid = row_slot.reshape(peers, my_rows)
    filled_grid = filled.reshape(peers, my_rows)
    owner_grid = slot_grid // local_count
    send_table = rank_table(filled_grid & (owner_grid == here), capacity)
    shrink_grid = shrink_local.reshape(peers, my_rows, -1)
    packed_shrink = jnp.einsum(
        "jkr,jra->jka", send_table, shrink_grid, preferred_element_type=jnp.float32
    ).astype(jnp.bfloat16)
    packed_delta = jnp.dot(
        packed_shrink.reshape(peers * capacity, -1),
        expand_local_blocks,
        preferred_element_type=jnp.float32,
    ).astype(jnp.bfloat16)
    arrived_rows = lax.all_to_all(
        packed_delta.reshape(peers, capacity, -1), "wide", split_axis=0, concat_axis=0, tiled=True
    )
    mine_owner = lax.dynamic_slice_in_dim(owner_grid, here, 1, 0)
    mine_filled = lax.dynamic_slice_in_dim(filled_grid, here, 1, 0)
    sources = jnp.arange(peers, dtype=jnp.int32)
    from_owner = mine_filled & (mine_owner == sources[:, None])
    incoming_table = rank_table(from_owner, capacity)
    adapter_update = jnp.einsum(
        "snh,sny->hy", incoming_table, arrived_rows, preferred_element_type=jnp.float32
    )
    base_token_rows = lax.all_to_all(base_cols, "wide", split_axis=0, concat_axis=1, tiled=True)
    return (base_token_rows + adapter_update).astype(jnp.bfloat16)


def solution(mesh):
    placed = (
        P(("groups", "wide"), None),
        P(None, "wide"),
        P("wide", None, None),
        P("wide", None, None),
        P(),
        P(("groups", "wide"), None),
        P(("groups", "wide"), None),
    )
    return jax.shard_map(
        body, mesh=mesh, in_specs=placed, out_specs=P(("groups", "wide"), None), check_vma=False
    )
```

profile of v0, /device:TPU:13, one launch (start us, length us, event | category | flops | bytes accessed | tf_op | source)
XLA Modules:
  0.0 334.8 jit_solution(1752114283837445706)
XLA Ops:
  6.5 0.0 copy-start
  6.5 0.0 all-gather.4.cloned.1.call-start
  6.5 0.7 all-gather.4.cloned.1.call-update
  7.3 15.6 %all-gather.1 = s32[16,1,4]{2,1,0:T(1,128)S(1)} all-gather(s32[1,1,4]{2,1,0:T(1,128)} %bitcast.41), channel_id=1, replica_groups=mesh['groups'=2,'wide'=16] {'wide'}, dimensions={0}, use_global_device_ids=true | all-gather | bytes 272 | tf_op jit(solution)/shard_map/all_gather | solution.py:16
  22.9 0.1 copy.29
  23.0 0.5 broadcast.343
  23.5 0.7 reduce.6
  24.2 21.5 %all-gather = s32[16,1,4]{2,1,0:T(1,128)S(1)} all-gather(s32[1,1,4]{2,1,0:T(1,128)} %bitcast.42), channel_id=1, replica_groups=mesh['groups'=2,'wide'=16] {'wide'}, dimensions={0}, use_global_device_ids=true | all-gather | bytes 272 | tf_op jit(solution)/shard_map/all_gather | solution.py:17
  45.7 0.1 copy.27
  45.7 0.7 reduce.7
  46.4 0.1 reshape.326
  46.5 0.1 broadcast_in_dim.40
  46.6 0.1 reshape.330
  46.7 0.1 reshape.327
  46.8 0.1 copy.30
  46.9 0.1 reshape.328
  47.0 0.1 copy.28
  47.1 0.0 copy-done
  47.1 1.9 gather_fusion
  49.0 0.1 gather.7
  49.0 0.1 broadcast_in_dim.42
  49.1 0.1 reshape.329
  49.3 35.2 %all-gather.4.cloned.1.call-done = bf16[256,16384]{1,0:T(8,128)(2,1)} async-done(((bf16[16,16384]{1,0:T(8,128)(2,1)}), bf16[256,16384]{1,0:T(8,128)(2,1)}) %all-gather.4.cloned.1.call-update) | async-done | bytes 8388624 | tf_op jit(solution)/shard_map/all_gather | solution.py:35
  84.5 18.2 %fusion.22 = f32[256,1024]{1,0:T(8,128)} fusion(bf16[256,16384]{1,0:T(8,128)(2,1)} %all-gather.4.cloned.1.call-done, bf16[16384,1024]{1,0:T(8,128)(2,1)} %param.8), kind=kOutput, calls=%fused_computation.50 | convolution fusion | flops 8589934592 | bytes 42991616 | tf_op jit(solution)/shard_map/dot_general | solution.py:36
  102.7 5.4 %all-to-all-start = ((f32[16,16,1024]{2,1,0:T(8,128)}), f32[16,16,1024]{2,1,0:T(8,128)S(1)}, u32[]{:S(2)}, u32[]{:S(2)}) async-start(f32[16,16,1024]{2,1,0:T(8,128)} %bitcast), calls=%async_computation | async-start | bytes 2097152 | tf_op jit(solution)/shard_map/all_to_all | solution.py:75
  108.2 0.2 reduce_window_sum.18
  108.3 6.9 %fusion.3 = bf16[256,128]{1,0:T(8,128)(2,1)S(1)} fusion(bf16[256,16384]{1,0:T(8,128)(2,1)} %all-gather.4.cloned.1.call-done, bf16[128,16384]{1,0:T(8,128)(2,1)} %bitcast.32, s32[128]{0:T(128)S(1)} %fusion.18, s32[256]{0:T(256)S(1)} %and_select_fusion.1, pred[256]{0:T(512)(128)(4,1)S(1)} %fusion.17), kind=kOutput, calls=%fused_computation.8 | convolution fusion | flops 1073872896 | bytes 12650240 | tf_op jit(solution)/shard_map/dot_general | solution.py:37
  115.2 0.2 convolution_convert_fusion.1
  115.4 6.7 %convolution_convert_fusion = bf16[192,16384]{1,0:T(8,128)(2,1)} fusion(bf16[192,128]{1,0:T(8,128)(2,1)S(1)} %reshape.333, bf16[128,16384]{1,0:T(8,128)(2,1)} %bitcast.31), kind=kOutput, calls=%fused_computation.1 | convolution fusion | flops 808452096 | bytes 10534912 | tf_op jit(solution)/shard_map/dot_general | solution.py:59
  122.1 8.6 %reshape.335 = bf16[16,12,16384]{2,1,0:T(8,128)(2,1)} reshape(bf16[192,16384]{1,0:T(8,128)(2,1)} %convolution_convert_fusion) | data formatting | bytes 12582912 | tf_op jit(solution)/shard_map/reshape | solution.py:65
  130.7 2.4 all-to-all-done
  133.0 4.9 %all-to-all-start.1 = ((bf16[16,12,16384]{2,1,0:T(8,128)(2,1)}), bf16[16,12,16384]{2,1,0:T(8,128)(2,1)}, u32[]{:S(2)}, u32[]{:S(2)}) async-start(bf16[16,12,16384]{2,1,0:T(8,128)(2,1)} %reshape.335), calls=%async_computation.1 | async-start | bytes 16777216 | tf_op jit(solution)/shard_map/all_to_all | solution.py:64
  137.9 0.0 copy-start.1
  138.0 0.1 copy.33
  138.1 0.2 reduce_window_sum.17
  138.3 0.1 copy.34
  138.3 0.1 copy.36
  138.5 181.8 %all-to-all-done.1 = bf16[16,12,16384]{2,1,0:T(8,128)(2,1)} async-done(((bf16[16,12,16384]{2,1,0:T(8,128)(2,1)}), bf16[16,12,16384]{2,1,0:T(8,128)(2,1)}, u32[]{:S(2)}, u32[]{:S(2)}) %all-to-all-start.1) | async-done | bytes 6291488 | tf_op jit(solution)/shard_map/all_to_all | solution.py:64
  320.3 7.7 %fusion.1 = bf16[16,16384]{1,0:T(8,128)(2,1)} fusion(f32[16,16384]{1,0:T(8,128)S(1)} %bitcast.34, bf16[16,12,16384]{2,1,0:T(8,128)(2,1)} %all-to-all-done.1, s32[16,16]{0,1:T(8,128)S(1)} %copy.34, pred[16,16]{0,1:T(8,128)(4,1)S(1)} %copy.33), kind=kOutput, calls=%fused_computation.4 | convolution fusion | flops 101193728 | bytes 7865600 | tf_op jit(solution)/shard_map/snh,sny->hy/dot_general | solution.py:72
  328.0 0.0 copy-done.1
  (14 shorter events, 0.1 us)
Async XLA Ops:
  6.5 40.5 %copy-start = (s32[128]{0:T(128)S(1)}, s32[128]{0:T(128)}, u32[]{:S(2)}) copy-start(s32[128]{0:T(128)} %param.11) | copy-start | bytes 1540
  6.5 78.0 %all-gather.4.cloned.1.call-start = ((), (), s32[]{:S(2)}) async-start(), calls=%async_computation.2 | async-start | bytes 8912896 | tf_op jit(solution)/shard_map/all_gather | solution.py:35
  102.7 30.3 %all-to-all-start = ((f32[16,16,1024]{2,1,0:T(8,128)}), f32[16,16,1024]{2,1,0:T(8,128)S(1)}, u32[]{:S(2)}, u32[]{:S(2)}) async-start(f32[16,16,1024]{2,1,0:T(8,128)} %bitcast), calls=%async_computation | async-start | bytes 2097152 | tf_op jit(solution)/shard_map/all_to_all | solution.py:75
  133.0 187.3 %all-to-all-start.1 = ((bf16[16,12,16384]{2,1,0:T(8,128)(2,1)}), bf16[16,12,16384]{2,1,0:T(8,128)(2,1)}, u32[]{:S(2)}, u32[]{:S(2)}) async-start(bf16[16,12,16384]{2,1,0:T(8,128)(2,1)} %reshape.335), calls=%async_computation.1 | async-start | bytes 16777216 | tf_op jit(solution)/shard_map/all_to_all | solution.py:64
  137.9 190.0 %copy-start.1 = (s32[128]{0:T(128)S(1)}, s32[128]{0:T(128)}, u32[]{:S(2)}) copy-start(s32[128]{0:T(128)} %param.11) | copy-start | bytes 1540
Sparse Core Ops, SparseCore 0:
  9.5 74.9 all-gather.3
where the time goes:
time: 335 us
  waiting for transfers between devices  220 us (66%)
  matrix products  39.6 us (12%)
  blocking collectives  37.1 us (11%)
  between operations  13.5 us (4%)
  local copies, waits for them, and re-layouts  12.3 us (4%)
  starting transfers between devices  10.3 us (3%)
    all_to_all x1, waiting for transfers between devices, body(): lax.all_to_all(packed_delta.reshape(peers, capacity, -1), 'wide', split_a...  182 us
    all_gather x1, waiting for transfers between devices, body(): block_rows = lax.all_gather(tokens, 'wide', axis=0, tiled=True)  35.2 us
    all_gather x1, blocking collectives, body(): lax.all_gather(seg_lengths, 'wide', axis=0, tiled=True)  21.5 us
    dot_general x1, matrix products, body(): jnp.dot(block_rows, base_weight, preferred_element_type=jnp.float32)  18.2 us
    all_gather x1, blocking collectives, body(): lax.all_gather(seg_adapter, 'wide', axis=0, tiled=True)  15.6 us
    reshape x1, local copies, waits for them, and re-layouts, body(): packed_delta.reshape(peers, capacity, -1)  8.58 us
    dot_general x1, matrix products, body(): jnp.einsum('snh,sny->hy', incoming_table, arrived_rows, preferred_element...  7.65 us
    dot_general x1, matrix products, body(): lax.dot_general(block_rows, shrink_local_blocks, (((1,), (1,)), ((), ()))...  6.89 us
  transfers between devices with their start and end apart: 3, of which 3 were waited for; matrix products, arithmetic and copies ran while one was open for 8% of the time, Pallas kernels for 0%

commit v1 on v0

v1 whole, which is shorter than its diff:
```python
import jax
import jax.numpy as jnp
from jax import lax
from jax.sharding import PartitionSpec as P


def body(tokens, base_weight, shrink_blocks, expand_blocks, adapter_slot, seg_adapter, seg_lengths):
    my_rows = tokens.shape[0]
    segment_cap = my_rows // seg_adapter.shape[1]
    local_count, rank_size, width = shrink_blocks.shape
    here = lax.axis_index("wide")
    peers = lax.axis_size("wide")
    position = jnp.arange(segment_cap, dtype=jnp.int32)
    my_slot = jnp.take(adapter_slot, seg_adapter.reshape(-1))
    my_row_slot = jnp.where(
        position[None, :] < seg_lengths.reshape(-1, 1), my_slot[:, None], -1
    ).reshape(1, my_rows)
    row_slot = lax.all_gather(my_row_slot, "wide", axis=0, tiled=True).reshape(-1)
    rows = lax.all_gather(tokens, "wide", axis=0, tiled=True)

    column_slot = (
        here * local_count + jnp.arange(local_count * rank_size, dtype=jnp.int32) // rank_size
    )
    selected = row_slot[:, None] == column_slot[None, :]
    shrink = lax.dot_general(
        rows,
        shrink_blocks.reshape(local_count * rank_size, width),
        (((1,), (1,)), ((), ())),
        preferred_element_type=jnp.float32,
    )
    shrink = jnp.where(selected, shrink, jnp.float32(0.0)).astype(jnp.bfloat16)
    delta = jnp.dot(
        shrink,
        expand_blocks.reshape(local_count * rank_size, width),
        preferred_element_type=jnp.float32,
    ).astype(jnp.bfloat16)
    update = lax.psum_scatter(delta, "wide", scatter_dimension=0, tiled=True)

    base = jnp.dot(rows, base_weight, preferred_element_type=jnp.float32).astype(jnp.bfloat16)
    base_rows = lax.all_to_all(
        base.reshape(peers, my_rows, -1), "wide", split_axis=0, concat_axis=0, tiled=True
    )
    base_rows = jnp.swapaxes(base_rows, 0, 1).reshape(my_rows, width)
    return (base_rows.astype(jnp.float32) + update.astype(jnp.float32)).astype(jnp.bfloat16)


def solution(mesh):
    placed = (
        P(("groups", "wide"), None),
        P(None, "wide"),
        P("wide", None, None),
        P("wide", None, None),
        P(),
        P(("groups", "wide"), None),
        P(("groups", "wide"), None),
    )
    return jax.shard_map(
        body, mesh=mesh, in_specs=placed, out_specs=P(("groups", "wide"), None), check_vma=False
    )
```

time: 335 us -> 224 us (0.67)
  waiting for transfers between devices: 220 us -> 121 us
  local copies, waits for them, and re-layouts: 12.3 us -> 1.39 us
  starting transfers between devices: 10.3 us -> 0.04 us
  blocking collectives: 37.1 us -> 43.6 us
    all_to_all x2 -> x0, waiting for transfers between devices: 184 us -> none  [the longest x1 182 us: body(): lax.all_to_all(packed_delta.reshape(peers, capacity, -1), 'wide', split_a...]
    reduce_scatter x0 -> x1, waiting for transfers between devices: none -> 62.5 us  [body(): update = lax.psum_scatter(delta, 'wide', scatter_dimension=0, tiled=True)]
    all_to_all x0 -> x1, blocking collectives: none -> 28.1 us  [body(): lax.all_to_all(base.reshape(peers, my_rows, -1), 'wide', split_axis=0, co...]
    all_gather x1, waiting for transfers between devices: 35.2 us -> 57.6 us  [body(): rows = lax.all_gather(tokens, 'wide', axis=0, tiled=True)]
    all_gather x2 -> x1, blocking collectives: 37.1 us -> 15.5 us  [body(): lax.all_gather(my_row_slot, 'wide', axis=0, tiled=True).reshape(-1)]
    all_to_all x2 -> x0, starting transfers between devices: 10.3 us -> none  [the longest x1 5.41 us: body(): lax.all_to_all(base_cols, 'wide', split_axis=0, concat_axis=1, tiled=True)]
    reshape x7 -> x0, local copies, waits for them, and re-layouts: 9.1 us -> none  [the longest x1 8.58 us: body(): packed_delta.reshape(peers, capacity, -1)]
    dot_general x5 -> x2, matrix products: 39.6 us -> 37.8 us  [the longest x1 19.8 us: body(): jnp.dot(rows, base_weight, preferred_element_type=jnp.float32)]
  transfers between devices with their start and end apart: 3 -> 2, of which waited for: 3 -> 2; matrix products, arithmetic and copies ran while one was open for 8% -> 11% of each run, Pallas kernels for 0% -> 0%
where the time goes in v1:
time: 224 us; the launch traced here: 222 us
  waiting for transfers between devices  121 us (54%)
  blocking collectives  43.6 us (19%)
  matrix products  37.8 us (17%)
  between operations  13.4 us (6%)
  other arithmetic  4.8 us (2%)
    reduce_scatter x1, waiting for transfers between devices, body(): update = lax.psum_scatter(delta, 'wide', scatter_dimension=0, tiled=True)  62.5 us
    all_gather x1, waiting for transfers between devices, body(): rows = lax.all_gather(tokens, 'wide', axis=0, tiled=True)  57.6 us
    all_to_all x1, blocking collectives, body(): lax.all_to_all(base.reshape(peers, my_rows, -1), 'wide', split_axis=0, co...  28.1 us
    dot_general x1, matrix products, body(): jnp.dot(rows, base_weight, preferred_element_type=jnp.float32)  19.8 us
    dot_general x1, matrix products, body(): jnp.dot(shrink, expand_blocks.reshape(local_count * rank_size, width), pr...  18 us
    all_gather x1, blocking collectives, body(): lax.all_gather(my_row_slot, 'wide', axis=0, tiled=True).reshape(-1)  15.5 us
  transfers between devices with their start and end apart: 2, of which 2 were waited for; matrix products, arithmetic and copies ran while one was open for 11% of the time, Pallas kernels for 0%

profile of v1, /device:TPU:13, one launch (start us, length us, event | category | flops | bytes accessed | tf_op | source)
XLA Modules:
  0.0 221.9 jit_solution(6631152067529117557)
XLA Ops:
  6.5 0.0 copy-start
  6.5 0.0 all-gather.3.cloned.1.call-start
  6.5 0.7 all-gather.3.cloned.1.call-update
  7.3 0.0 reduce-scatter.2.cloned.1.call-start
  7.3 0.7 fusion.3
  8.0 0.0 copy-done
  8.0 0.6 gather_fusion
  8.6 0.7 and_select_fusion.1
  9.3 0.7 fusion.1
  10.0 0.1 reshape.132
  10.1 15.5 %all-gather = s32[16,1,16]{2,1,0:T(1,128)S(1)} all-gather(s32[1,1,16]{2,1,0:T(1,128)S(1)} %reshape.132), channel_id=1, replica_groups=mesh['groups'=2,'wide'=16] {'wide'}, dimensions={0}, use_global_device_ids=true | all-gather | bytes 1088 | tf_op jit(solution)/shard_map/all_gather | solution.py:18
  25.6 0.5 broadcast.107
  26.1 0.7 reduce.3
  26.8 0.1 eq.15
  26.8 57.6 %all-gather.3.cloned.1.call-done = bf16[256,16384]{1,0:T(8,128)(2,1)} async-done(((bf16[16,16384]{1,0:T(8,128)(2,1)}), bf16[256,16384]{1,0:T(8,128)(2,1)}) %all-gather.3.cloned.1.call-update) | async-done | bytes 8388624 | tf_op jit(solution)/shard_map/all_gather | solution.py:19
  84.5 18.0 %convolution_convert_fusion = bf16[256,16384]{1,0:T(8,128)(2,1)} fusion(bf16[128,16384]{1,0:T(8,128)(2,1)} %bitcast.29, bf16[256,16384]{1,0:T(8,128)(2,1)} %all-gather.3.cloned.1.call-done, bf16[128,16384]{1,0:T(8,128)(2,1)} %bitcast.28, s32[128]{0:T(128)S(1)} %fusion.2, s32[256]{0:T(256)S(1)} %eq.15), kind=kOutput, calls=%fused_computation.1 | convolution fusion | flops 2151776256 | bytes 25167360 | tf_op jit(solution)/shard_map/dot_general | solution.py:32
  102.4 0.0 reduce-scatter.2.cloned.1.call-update
  102.5 19.8 %convolution_convert_fusion.1 = bf16[256,1024]{1,0:T(8,128)(2,1)S(1)} fusion(bf16[256,16384]{1,0:T(8,128)(2,1)} %all-gather.3.cloned.1.call-done, bf16[16384,1024]{1,0:T(8,128)(2,1)} %param.8), kind=kOutput, calls=%fused_computation.2 | convolution fusion | flops 8590196736 | bytes 42467328 | tf_op jit(solution)/shard_map/dot_general | solution.py:39
  122.3 28.1 %all_to_all.5 = bf16[16,16,1024]{2,1,0:T(8,128)(2,1)S(1)} all-to-all(bf16[16,16,1024]{2,1,0:T(8,128)(2,1)S(1)} %bitcast.31), channel_id=1, replica_groups=mesh['groups'=2,'wide'=16] {'wide'}, dimensions={0} | all-to-all | bytes 1048576 | tf_op jit(solution)/shard_map/all_to_all | solution.py:40
  150.4 0.1 convert_bitcast_fusion
  150.5 0.1 copy.11
  150.6 62.5 %reduce-scatter.2.cloned.1.call-done = bf16[16,16384]{1,0:T(8,128)(2,1)} async-done(((bf16[256,16384]{1,0:T(8,128)(2,1)}), bf16[16,16384]{1,0:T(8,128)(2,1)}) %reduce-scatter.2.cloned.1.call-update) | async-done | bytes 524304 | tf_op jit(solution)/shard_map/reduce_scatter | solution.py:37
  213.1 2.0 add_convert_fusion
  (2 shorter events, 0.0 us)
Async XLA Ops:
  6.5 1.4 copy-start
  6.5 78.0 %all-gather.3.cloned.1.call-start = ((), (), s32[]{:S(2)}) async-start(), calls=%async_computation.2 | async-start | bytes 8912896 | tf_op jit(solution)/shard_map/all_gather | solution.py:19
  7.3 205.9 %reduce-scatter.2.cloned.1.call-start = ((), (), s32[]{:S(2)}) async-start(), calls=%async_computation.3 | async-start | bytes 8912896 | tf_op jit(solution)/shard_map/reduce_scatter | solution.py:37
Sparse Core Ops, SparseCore 0:
  9.5 74.9 all-gather.2
  102.6 110.4 reduce-scatter.1

commit v2 on v1

--- a/solution.py
+++ b/solution.py
@@ -1,10 +1,145 @@
+import functools
+
 import jax
 import jax.numpy as jnp
 from jax import lax
+from jax.experimental import pallas as pl
+from jax.experimental.pallas import tpu as pltpu
 from jax.sharding import PartitionSpec as P
 
 
-def body(tokens, base_weight, shrink_blocks, expand_blocks, adapter_slot, seg_adapter, seg_lengths):
+CHUNKS = 4
+MESH = pl.DeviceIdType.MESH
+
+
+def ring(n, snake):
+    me = lax.axis_index("wide")
+    chips = n // 2
+    core, chip = me % 2, me // 2
+    half = chips // 2
+
+    def device(position, on_core):
+        at = (position + chips) % chips
+        if snake:
+            back = at // half
+            at = (1 - back) * (2 * at) + back * (2 * (chips - 1 - at) + 1)
+        return at * 2 + on_core
+
+    position = chip
+    if snake:
+        low, high = chip % 2, chip // 2
+        position = (1 - low) * high + low * (chips - 1 - high)
+    return me, core, position, device
+
+
+def greet_all(n, me):
+    barrier = pltpu.get_barrier_semaphore()
+    for step in range(1, n):
+        pl.semaphore_signal(
+            barrier, inc=1, device_id={"wide": (me + step) % n}, device_id_type=MESH
+        )
+    pl.semaphore_wait(barrier, n - 1)
+
+
+def gather_kernel(
+    n, snake, tok, meta, out, meta_out, own_sem, meta_send, meta_recv,
+    right_send, right_recv, left_send, left_recv, sib_send, sib_recv,
+):
+    me, core, position, device = ring(n, snake)
+    chips = n // 2
+    rows, width = tok.shape
+    part = width // CHUNKS
+    right_hops = chips // 2
+    left_hops = chips - 1 - right_hops
+    right, left, sibling = device(position + 1, core), device(position - 1, core), device(position, 1 - core)
+    greet_all(n, me)
+
+    def place(owner, k):
+        return out.at[pl.ds(pl.multiple_of(owner * rows, rows), rows), pl.ds(k * part, part)]
+
+    def copy(src, dst, send, recv, target):
+        return pltpu.make_async_remote_copy(
+            src_ref=src, dst_ref=dst, send_sem=send, recv_sem=recv,
+            device_id={"wide": target}, device_id_type=MESH,
+        )
+
+    started = []
+    for k in range(CHUNKS):
+        src = tok.at[:, pl.ds(k * part, part)]
+        started.append(copy(src, place(me, k), right_send.at[0, k], right_recv.at[0, k], right))
+        started[-1].start()
+        started.append(copy(src, place(me, k), left_send.at[0, k], left_recv.at[0, k], left))
+        started[-1].start()
+    for step in range(1, n):
+        started.append(
+            copy(meta, meta_out.at[me], meta_send.at[step], meta_recv.at[step], (me + step) % n)
+        )
+        started[-1].start()
+    for k in range(CHUNKS):
+        src = tok.at[:, pl.ds(k * part, part)]
+        started.append(copy(src, place(me, k), sib_send.at[0, k], sib_recv.at[0, k], sibling))
+        started[-1].start()
+    own_rows = pltpu.make_async_copy(tok, out.at[pl.ds(pl.multiple_of(me * rows, rows), rows), :], own_sem.at[0])
+    own_meta = pltpu.make_async_copy(meta, meta_out.at[me], own_sem.at[1])
+    own_rows.start()
+    own_meta.start()
+
+    for hop in range(1, right_hops + 1):
+        for k in range(CHUNKS):
+            block = place(device(position - hop, core), k)
+            copy(block, block, right_send.at[hop - 1, k], right_recv.at[hop - 1, k], right).wait_recv()
+            if hop < right_hops:
+                started.append(copy(block, block, right_send.at[hop, k], right_recv.at[hop, k], right))
+                started[-1].start()
+            started.append(copy(block, block, sib_send.at[hop, k], sib_recv.at[hop, k], sibling))
+            started[-1].start()
+            if hop <= left_hops:
+                block = place(device(position + hop, core), k)
+                copy(block, block, left_send.at[hop - 1, k], left_recv.at[hop - 1, k], left).wait_recv()
+                if hop < left_hops:
+                    started.append(copy(block, block, left_send.at[hop, k], left_recv.at[hop, k], left))
+                    started[-1].start()
+                at = right_hops + hop
+                started.append(copy(block, block, sib_send.at[at, k], sib_recv.at[at, k], sibling))
+                started[-1].start()
+
+    for at in range(chips):
+        source = position - at if at <= right_hops else position + at - right_hops
+        for k in range(CHUNKS):
+            block = place(device(source, 1 - core), k)
+            copy(block, block, sib_send.at[at, k], sib_recv.at[at, k], sibling).wait_recv()
+    for step in range(1, n):
+        dst = meta_out.at[(me - step + n) % n]
+        copy(meta, dst, meta_send.at[step], meta_recv.at[step], (me + step) % n).wait_recv()
+    for one in started:
+        one.wait_send()
+    own_rows.wait()
+    own_meta.wait()
+
+
+def gather(tokens, meta, n, snake):
+    rows, width = tokens.shape
+    chips = n // 2
+    hops = chips // 2
+    dma = pltpu.SemaphoreType.DMA
+    return pl.pallas_call(
+        functools.partial(gather_kernel, n, snake),
+        out_shape=(
+            jax.ShapeDtypeStruct((n * rows, width), tokens.dtype),
+            jax.ShapeDtypeStruct((n,) + meta.shape, meta.dtype),
+        ),
+        in_specs=[pl.BlockSpec(memory_space=pl.ANY)] * 2,
+        out_specs=(pl.BlockSpec(memory_space=pl.ANY),) * 2,
+        scratch_shapes=[
+            dma((2,)), dma((n,)), dma((n,)),
+            dma((hops, CHUNKS)), dma((hops, CHUNKS)), dma((hops, CHUNKS)), dma((hops, CHUNKS)),
+            dma((chips, CHUNKS)), dma((chips, CHUNKS)),
+        ],
+        compiler_params=pltpu.CompilerParams(collective_id=0, has_side_effects=True),
+    )(tokens, meta)
+
+
+def body(snake, tokens, base_weight, shrink_blocks, expand_blocks, adapter_slot, seg_adapter, seg_lengths):
     my_rows = tokens.shape[0]
     segment_cap = my_rows // seg_adapter.shape[1]
     local_count, rank_size, width = shrink_blocks.shape
@@ -15,8 +150,9 @@
     my_row_slot = jnp.where(
         position[None, :] < seg_lengths.reshape(-1, 1), my_slot[:, None], -1
     ).reshape(1, my_rows)
-    row_slot = lax.all_gather(my_row_slot, "wide", axis=0, tiled=True).reshape(-1)
-    rows = lax.all_gather(tokens, "wide", axis=0, tiled=True)
+    meta = jnp.broadcast_to(jnp.pad(my_row_slot, ((0, 0), (0, 128 - my_rows))), (8, 128))
+    rows, meta_all = gather(tokens, meta, peers, snake)
+    row_slot = meta_all[:, 0, :my_rows].reshape(-1)
 
     column_slot = (
         here * local_count + jnp.arange(local_count * rank_size, dtype=jnp.int32) // rank_size
@@ -54,6 +190,7 @@
         P(("groups", "wide"), None),
         P(("groups", "wide"), None),
     )
+    snake = mesh.shape["groups"] == 2
     return jax.shard_map(
-        body, mesh=mesh, in_specs=placed, out_specs=P(("groups", "wide"), None), check_vma=False
+        functools.partial(body, snake), mesh=mesh, in_specs=placed, out_specs=P(("groups", "wide"), None), check_vma=False
     )

time: 224 us -> 204 us (0.911)
  waiting for transfers between devices: 121 us -> 63 us
  Pallas kernels: 0 us -> 54.3 us
  blocking collectives: 43.6 us -> 27.7 us
    all_gather x1 -> x0, waiting for transfers between devices: 57.6 us -> none  [body(): rows = lax.all_gather(tokens, 'wide', axis=0, tiled=True)]
    pallas_call x0 -> x1, Pallas kernels: none -> 54.3 us  [gather(): pl.pallas_call(functools.partial(gather_kernel, n, snake), out_shape=(jax...]
    all_gather x1 -> x0, blocking collectives: 15.5 us -> none  [body(): lax.all_gather(my_row_slot, 'wide', axis=0, tiled=True).reshape(-1)]
  transfers between devices with their start and end apart: 2 -> 1, of which waited for: 2 -> 1; matrix products, arithmetic and copies ran while one was open for 11% -> 10% of each run, Pallas kernels for 0% -> 0%
where the time goes in v2:
time: 204 us; the launch traced here: 203 us
  waiting for transfers between devices  63 us (31%)
  Pallas kernels  54.3 us (27%)
  matrix products  37.7 us (18%)
  blocking collectives  27.7 us (14%)
  between operations  13.4 us (7%)
  other arithmetic  4.14 us (2%)
  local copies, waits for them, and re-layouts  2.35 us (1%)
    reduce_scatter x1, waiting for transfers between devices, body(): update = lax.psum_scatter(delta, 'wide', scatter_dimension=0, tiled=True)  63 us
    pallas_call x1, Pallas kernels, gather(): pl.pallas_call(functools.partial(gather_kernel, n, snake), out_shape=(jax...  54.3 us
    all_to_all x1, blocking collectives, body(): lax.all_to_all(base.reshape(peers, my_rows, -1), 'wide', split_axis=0, co...  27.7 us
    dot_general x1, matrix products, body(): jnp.dot(rows, base_weight, preferred_element_type=jnp.float32)  19.8 us
    dot_general x1, matrix products, body(): jnp.dot(shrink, expand_blocks.reshape(local_count * rank_size, width), pr...  17.9 us
  transfers between devices with their start and end apart: 1, of which 1 were waited for; matrix products, arithmetic and copies ran while one was open for 10% of the time, Pallas kernels for 0%

profile of v2, /device:TPU:13, one launch (start us, length us, event | category | flops | bytes accessed | tf_op | source)
XLA Modules:
  0.0 202.6 jit_solution(8262358230281901098)
XLA Ops:
  6.5 0.0 copy-start
  6.5 0.0 reduce-scatter.2.cloned.1.call-start
  6.5 0.7 fusion.3
  7.2 0.0 copy-done
  7.2 0.6 gather_fusion
  7.9 0.7 and_select_fusion.1
  8.5 0.7 fusion.1
  9.2 0.1 select_n.58
  9.3 0.6 broadcast_in_dim.31.meta
  9.9 54.3 %shard_map.73 = (bf16[256,16384]{1,0:T(8,128)(2,1)}, s32[16,8,128]{2,1,0:T(8,128)}) custom-call(bf16[16,16384]{1,0:T(8,128)(2,1)} %tok.1, s32[8,128]{1,0:T(8,128)} %broadcast_in_dim.31.meta), custom_call_target="tpu_custom_call" | custom-call | tf_op jit(solution)/shard_map/pallas_call | solution.py:125
  64.2 0.9 slice_reduce_fusion
  65.1 0.1 eq.15
  65.2 17.9 %convolution_convert_fusion = bf16[256,16384]{1,0:T(8,128)(2,1)} fusion(bf16[128,16384]{1,0:T(8,128)(2,1)} %bitcast.31, bf16[256,16384]{1,0:T(8,128)(2,1)} %get-tuple-element.7, bf16[128,16384]{1,0:T(8,128)(2,1)} %bitcast.30, s32[128]{0:T(128)S(1)} %fusion.2, s32[256]{0:T(256)S(1)} %eq.15), kind=kOutput, calls=%fused_computation.1 | convolution fusion | flops 2151776256 | bytes 25167360 | tf_op jit(solution)/shard_map/dot_general | solution.py:168
  83.1 0.0 reduce-scatter.2.cloned.1.call-update
  83.2 19.8 %convolution_convert_fusion.1 = bf16[256,1024]{1,0:T(8,128)(2,1)S(1)} fusion(bf16[256,16384]{1,0:T(8,128)(2,1)} %get-tuple-element.7, bf16[16384,1024]{1,0:T(8,128)(2,1)} %param.8), kind=kOutput, calls=%fused_computation.2 | convolution fusion | flops 8590196736 | bytes 42467328 | tf_op jit(solution)/shard_map/dot_general | solution.py:175
  102.9 27.7 %all_to_all.5 = bf16[16,16,1024]{2,1,0:T(8,128)(2,1)S(1)} all-to-all(bf16[16,16,1024]{2,1,0:T(8,128)(2,1)S(1)} %bitcast.33), channel_id=1, replica_groups=mesh['groups'=2,'wide'=16] {'wide'}, dimensions={0} | all-to-all | bytes 1048576 | tf_op jit(solution)/shard_map/all_to_all | solution.py:176
  130.6 0.1 convert_bitcast_fusion
  130.8 0.1 copy.10
  130.8 63.0 %reduce-scatter.2.cloned.1.call-done = bf16[16,16384]{1,0:T(8,128)(2,1)} async-done(((bf16[256,16384]{1,0:T(8,128)(2,1)}), bf16[16,16384]{1,0:T(8,128)(2,1)}) %reduce-scatter.2.cloned.1.call-update) | async-done | bytes 524304 | tf_op jit(solution)/shard_map/reduce_scatter | solution.py:173
  193.8 2.0 add_convert_fusion
  (3 shorter events, 0.0 us)
Async XLA Ops:
  6.5 0.7 copy-start
  6.5 187.3 %reduce-scatter.2.cloned.1.call-start = ((), (), s32[]{:S(2)}) async-start(), calls=%async_computation.2 | async-start | bytes 8912896 | tf_op jit(solution)/shard_map/reduce_scatter | solution.py:173
Sparse Core Ops, SparseCore 0:
  83.3 110.5 reduce-scatter.1

commit v3 on v2

--- a/solution.py
+++ b/solution.py
@@ -139,6 +139,141 @@
     )(tokens, meta)
 
 
+def reduce_kernel(
+    n, snake, delta, base, out, sib, from_left, from_right, pieces, base_send, base_recv,
+    right_send, right_recv, left_send, left_recv, sib_send, sib_recv,
+):
+    me, core, position, device = ring(n, snake)
+    chips = n // 2
+    rows, width = out.shape
+    part, piece = width // CHUNKS, width // n
+    right_hops = chips // 2
+    left_hops = chips - 1 - right_hops
+    right, left, sibling = device(position + 1, core), device(position - 1, core), device(position, 1 - core)
+    offsets = []
+    for hop in range(right_hops):
+        offsets.append(right_hops - hop)
+        if hop < left_hops:
+            offsets.append(hop - left_hops)
+    offsets.append(0)
+    greet_all(n, me)
+
+    def block(owner):
+        return pl.ds(pl.multiple_of(owner * rows, rows), rows)
+
+    def columns(k):
+        return pl.ds(k * part, part)
+
+    def copy(src, dst, send, recv, target):
+        return pltpu.make_async_remote_copy(
+            src_ref=src, dst_ref=dst, send_sem=send, recv_sem=recv,
+            device_id={"wide": target}, device_id_type=MESH,
+        )
+
+    def sib_copy(j, k):
+        return copy(
+            delta.at[block(device(position + offsets[j], 1 - core)), columns(k)],
+            sib.at[j, :, columns(k)], sib_send.at[j, k], sib_recv.at[j, k], sibling,
+        )
+
+    def chip_sum(offset, k):
+        j = offsets.index(offset)
+        sib_copy(j, k).wait_recv()
+        return sib[j, :, columns(k)] + delta[block(device(position + offset, core)), columns(k)]
+
+    def base_copy(step):
+        peer = (me + step) % n
+        return copy(base.at[block(peer), :], pieces.at[me], base_send.at[step], base_recv.at[step], peer)
+
+    started = []
+
+    def start(one):
+        one.start()
+        started.append(one)
+
+    def to_right(src, slot, k):
+        start(copy(src, from_left.at[slot, :, columns(k)], right_send.at[slot, k], right_recv.at[slot, k], right))
+
+    def to_left(src, slot, k):
+        start(copy(src, from_right.at[slot, :, columns(k)], left_send.at[slot, k], left_recv.at[slot, k], left))
+
+    for j in range(chips):
+        for k in range(CHUNKS):
+            start(sib_copy(j, k))
+    for k in range(CHUNKS):
+        j = offsets.index(right_hops)
+        sib[j, :, columns(k)] = chip_sum(right_hops, k)
+        to_right(sib.at[j, :, columns(k)], 0, k)
+    for k in range(CHUNKS):
+        j = offsets.index(-left_hops)
+        sib[j, :, columns(k)] = chip_sum(-left_hops, k)
+        to_left(sib.at[j, :, columns(k)], 0, k)
+    for step in range(1, n):
+        start(base_copy(step))
+    pieces[me] = base[block(me), :]
+
+    def right_arrival(slot, k):
+        here = from_left.at[slot, :, columns(k)]
+        copy(here, here, right_send.at[slot, k], right_recv.at[slot, k], right).wait_recv()
+
+    def left_arrival(slot, k):
+        here = from_right.at[slot, :, columns(k)]
+        copy(here, here, left_send.at[slot, k], left_recv.at[slot, k], left).wait_recv()
+
+    for hop in range(1, right_hops):
+        for k in range(CHUNKS):
+            own = chip_sum(right_hops - hop, k)
+            right_arrival(hop - 1, k)
+            from_left[hop - 1, :, columns(k)] = from_left[hop - 1, :, columns(k)] + own
+            to_right(from_left.at[hop - 1, :, columns(k)], hop, k)
+            if hop < left_hops:
+                own = chip_sum(hop - left_hops, k)
+                left_arrival(hop - 1, k)
+                from_right[hop - 1, :, columns(k)] = from_right[hop - 1, :, columns(k)] + own
+                to_left(from_right.at[hop - 1, :, columns(k)], hop, k)
+
+    for step in range(1, n):
+        sender = (me - step + n) % n
+        copy(
+            base.at[block(sender), :], pieces.at[sender], base_send.at[step], base_recv.at[step], sender
+        ).wait_recv()
+    for k in range(CHUNKS):
+        own = chip_sum(0, k)
+        left_arrival(left_hops - 1, k)
+        right_arrival(right_hops - 1, k)
+        update = own + from_right[left_hops - 1, :, columns(k)] + from_left[right_hops - 1, :, columns(k)]
+        per = n // CHUNKS
+        for d in range(per):
+            at = k * per + d
+            total = pieces[at].astype(jnp.float32) + update[:, d * piece:(d + 1) * piece].astype(jnp.float32)
+            out[:, at * piece:(at + 1) * piece] = total.astype(out.dtype)
+    for one in started:
+        one.wait_send()
+
+
+def reduce_rows(delta, base, n, snake):
+    rows, width = delta.shape[0] // n, delta.shape[1]
+    chips = n // 2
+    hops = chips // 2
+    dma = pltpu.SemaphoreType.DMA
+    slots = lambda count: pltpu.VMEM((count, rows, width), delta.dtype)
+    return pl.pallas_call(
+        functools.partial(reduce_kernel, n, snake),
+        out_shape=jax.ShapeDtypeStruct((rows, width), jnp.bfloat16),
+        in_specs=[pl.BlockSpec(memory_space=pltpu.VMEM)] * 2,
+        out_specs=pl.BlockSpec(memory_space=pltpu.VMEM),
+        scratch_shapes=[
+            slots(chips), slots(hops), slots(hops), pltpu.VMEM((n, rows, width // n), base.dtype),
+            dma((n,)), dma((n,)),
+            dma((hops, CHUNKS)), dma((hops, CHUNKS)), dma((hops, CHUNKS)), dma((hops, CHUNKS)),
+            dma((chips, CHUNKS)), dma((chips, CHUNKS)),
+        ],
+        compiler_params=pltpu.CompilerParams(
+            collective_id=1, has_side_effects=True, vmem_limit_bytes=52 * 1024 * 1024
+        ),
+    )(delta, base)
+
+
 def body(snake, tokens, base_weight, shrink_blocks, expand_blocks, adapter_slot, seg_adapter, seg_lengths):
     my_rows = tokens.shape[0]
     segment_cap = my_rows // seg_adapter.shape[1]
@@ -170,14 +305,8 @@
         expand_blocks.reshape(local_count * rank_size, width),
         preferred_element_type=jnp.float32,
     ).astype(jnp.bfloat16)
-    update = lax.psum_scatter(delta, "wide", scatter_dimension=0, tiled=True)
-
     base = jnp.dot(rows, base_weight, preferred_element_type=jnp.float32).astype(jnp.bfloat16)
-    base_rows = lax.all_to_all(
-        base.reshape(peers, my_rows, -1), "wide", split_axis=0, concat_axis=0, tiled=True
-    )
-    base_rows = jnp.swapaxes(base_rows, 0, 1).reshape(my_rows, width)
-    return (base_rows.astype(jnp.float32) + update.astype(jnp.float32)).astype(jnp.bfloat16)
+    return reduce_rows(delta, base, peers, snake)
 
 
 def solution(mesh):

time: 204 us -> 161 us (0.79)
  Pallas kernels: 54.3 us -> 121 us
  waiting for transfers between devices: 63 us -> 0 us
  blocking collectives: 27.7 us -> 0 us
  between operations: 13.4 us -> 0.04 us
  matrix products: 37.7 us -> 35.4 us
  other arithmetic: 4.14 us -> 2.07 us
    pallas_call x0 -> x1, Pallas kernels: none -> 66.3 us  [reduce_rows(): pl.pallas_call(functools.partial(reduce_kernel, n, snake), out_shape=jax....]
    reduce_scatter x1 -> x0, waiting for transfers between devices: 63 us -> none  [body(): update = lax.psum_scatter(delta, 'wide', scatter_dimension=0, tiled=True)]
    all_to_all x1 -> x0, blocking collectives: 27.7 us -> none  [body(): lax.all_to_all(base.reshape(peers, my_rows, -1), 'wide', split_axis=0, co...]
    dot_general x1, matrix products: 19.8 us -> 17.4 us  [body(): jnp.dot(rows, base_weight, preferred_element_type=jnp.float32)]
  transfers between devices with their start and end apart: 1 -> 0, of which waited for: 1 -> 0; matrix products, arithmetic and copies ran while one was open for 10% -> 0% of each run, Pallas kernels for 0% -> 0%
where the time goes in v3:
time: 161 us
  Pallas kernels  121 us (75%)
  matrix products  35.4 us (22%)
  local copies, waits for them, and re-layouts  3.07 us (2%)
  other arithmetic  2.07 us (1%)
    pallas_call x1, Pallas kernels, reduce_rows(): pl.pallas_call(functools.partial(reduce_kernel, n, snake), out_shape=jax....  66.3 us
    pallas_call x1, Pallas kernels, gather(): pl.pallas_call(functools.partial(gather_kernel, n, snake), out_shape=(jax...  54.3 us
    dot_general x1, matrix products, body(): jnp.dot(shrink, expand_blocks.reshape(local_count * rank_size, width), pr...  17.9 us
    dot_general x1, matrix products, body(): jnp.dot(rows, base_weight, preferred_element_type=jnp.float32)  17.4 us

profile of v3, /device:TPU:13, one launch (start us, length us, event | category | flops | bytes accessed | tf_op | source)
XLA Modules:
  0.0 161.2 jit_solution(16618060942496210724)
XLA Ops:
  0.0 0.0 copy-start
  0.0 0.7 fusion.3
  0.7 0.0 copy-done
  0.7 0.6 gather_fusion
  1.3 0.7 and_select_fusion.1
  2.0 0.7 fusion.1
  2.7 0.1 select_n.58
  2.8 0.6 broadcast_in_dim.31.meta
  3.4 54.3 %shard_map.73 = (bf16[256,16384]{1,0:T(8,128)(2,1)}, s32[16,8,128]{2,1,0:T(8,128)}) custom-call(bf16[16,16384]{1,0:T(8,128)(2,1)} %tok.1, s32[8,128]{1,0:T(8,128)} %broadcast_in_dim.31.meta), custom_call_target="tpu_custom_call" | custom-call | tf_op jit(solution)/shard_map/pallas_call | solution.py:125
  57.7 0.9 slice_reduce_fusion
  58.6 0.1 eq.15
  58.6 17.9 %convolution_convert_fusion.delta = bf16[256,16384]{1,0:T(8,128)(2,1)} fusion(bf16[128,16384]{1,0:T(8,128)(2,1)} %bitcast.26, bf16[256,16384]{1,0:T(8,128)(2,1)} %get-tuple-element.8, bf16[128,16384]{1,0:T(8,128)(2,1)} %bitcast.25, s32[128]{0:T(128)S(1)} %fusion.2, s32[256]{0:T(256)S(1)} %eq.15), kind=kOutput, calls=%fused_computation.1 | convolution fusion | flops 2151776256 | bytes 25167360 | tf_op jit(solution)/shard_map/dot_general | solution.py:303
  76.6 17.4 %convolution_convert_fusion.1.base = bf16[256,1024]{1,0:T(8,128)(2,1)S(1)} fusion(bf16[256,16384]{1,0:T(8,128)(2,1)} %get-tuple-element.8, bf16[16384,1024]{1,0:T(8,128)(2,1)} %param.8), kind=kOutput, calls=%fused_computation.2 | convolution fusion | flops 8590196736 | bytes 42467328 | tf_op jit(solution)/shard_map/dot_general | solution.py:308
  94.0 66.3 %shard_map.74 = bf16[16,16384]{1,0:T(8,128)(2,1)S(1)} custom-call(bf16[256,16384]{1,0:T(8,128)(2,1)} %convolution_convert_fusion.delta, bf16[256,1024]{1,0:T(8,128)(2,1)S(1)} %convolution_convert_fusion.1.base), custom_call_target="tpu_custom_call" | custom-call | tf_op jit(solution)/shard_map/pallas_call | solution.py:260
  160.4 0.8 copy.9
  (3 shorter events, 0.0 us)
Async XLA Ops:
  0.0 0.7 copy-start

commit v4 on v3

--- a/solution.py
+++ b/solution.py
@@ -84,22 +84,29 @@
     own_rows.start()
     own_meta.start()
 
+    def by_right(hop, k):
+        return hop < right_hops or (hop == right_hops and k < CHUNKS // 2)
+
+    def by_left(hop, k):
+        return hop <= left_hops or (hop == right_hops and k >= CHUNKS // 2)
+
     for hop in range(1, right_hops + 1):
         for k in range(CHUNKS):
-            block = place(device(position - hop, core), k)
-            copy(block, block, right_send.at[hop - 1, k], right_recv.at[hop - 1, k], right).wait_recv()
-            if hop < right_hops:
-                started.append(copy(block, block, right_send.at[hop, k], right_recv.at[hop, k], right))
+            if by_right(hop, k):
+                block = place(device(position - hop, core), k)
+                copy(block, block, right_send.at[hop - 1, k], right_recv.at[hop - 1, k], right).wait_recv()
+                if by_right(hop + 1, k):
+                    started.append(copy(block, block, right_send.at[hop, k], right_recv.at[hop, k], right))
+                    started[-1].start()
+                started.append(copy(block, block, sib_send.at[hop, k], sib_recv.at[hop, k], sibling))
                 started[-1].start()
-            started.append(copy(block, block, sib_send.at[hop, k], sib_recv.at[hop, k], sibling))
-            started[-1].start()
-            if hop <= left_hops:
+            if by_left(hop, k):
                 block = place(device(position + hop, core), k)
                 copy(block, block, left_send.at[hop - 1, k], left_recv.at[hop - 1, k], left).wait_recv()
-                if hop < left_hops:
+                if by_left(hop + 1, k):
                     started.append(copy(block, block, left_send.at[hop, k], left_recv.at[hop, k], left))
                     started[-1].start()
-                at = right_hops + hop
+                at = right_hops + hop if hop <= left_hops else hop
                 started.append(copy(block, block, sib_send.at[at, k], sib_recv.at[at, k], sibling))
                 started[-1].start()
 

time: 161 us -> 156 us (0.969)
  Pallas kernels: 121 us -> 115 us
    pallas_call x1, Pallas kernels: 54.3 us -> 49.2 us  [gather(): pl.pallas_call(functools.partial(gather_kernel, n, snake), out_shape=(jax...]
where the time goes in v4:
time: 156 us
  Pallas kernels  115 us (74%)
  matrix products  35.4 us (23%)
  local copies, waits for them, and re-layouts  3.07 us (2%)
  other arithmetic  2.07 us (1%)
    pallas_call x1, Pallas kernels, reduce_rows(): pl.pallas_call(functools.partial(reduce_kernel, n, snake), out_shape=jax....  66.1 us
    pallas_call x1, Pallas kernels, gather(): pl.pallas_call(functools.partial(gather_kernel, n, snake), out_shape=(jax...  49.2 us
    dot_general x1, matrix products, body(): jnp.dot(shrink, expand_blocks.reshape(local_count * rank_size, width), pr...  17.9 us
    dot_general x1, matrix products, body(): jnp.dot(rows, base_weight, preferred_element_type=jnp.float32)  17.4 us

profile of v4, /device:TPU:13, one launch (start us, length us, event | category | flops | bytes accessed | tf_op | source)
XLA Modules:
  0.0 155.9 jit_solution(14070005061426313406)
XLA Ops:
  0.0 0.0 copy-start
  0.0 0.7 fusion.3
  0.7 0.0 copy-done
  0.7 0.6 gather_fusion
  1.3 0.7 and_select_fusion.1
  2.0 0.7 fusion.1
  2.7 0.1 select_n.58
  2.8 0.6 broadcast_in_dim.31.meta
  3.4 49.2 %shard_map.73 = (bf16[256,16384]{1,0:T(8,128)(2,1)}, s32[16,8,128]{2,1,0:T(8,128)}) custom-call(bf16[16,16384]{1,0:T(8,128)(2,1)} %tok.1, s32[8,128]{1,0:T(8,128)} %broadcast_in_dim.31.meta), custom_call_target="tpu_custom_call" | custom-call | tf_op jit(solution)/shard_map/pallas_call | solution.py:132
  52.7 0.9 slice_reduce_fusion
  53.5 0.1 eq.15
  53.6 17.9 %convolution_convert_fusion.delta = bf16[256,16384]{1,0:T(8,128)(2,1)} fusion(bf16[128,16384]{1,0:T(8,128)(2,1)} %bitcast.26, bf16[256,16384]{1,0:T(8,128)(2,1)} %get-tuple-element.8, bf16[128,16384]{1,0:T(8,128)(2,1)} %bitcast.25, s32[128]{0:T(128)S(1)} %fusion.2, s32[256]{0:T(256)S(1)} %eq.15), kind=kOutput, calls=%fused_computation.1 | convolution fusion | flops 2151776256 | bytes 25167360 | tf_op jit(solution)/shard_map/dot_general | solution.py:310
  71.6 17.4 %convolution_convert_fusion.1.base = bf16[256,1024]{1,0:T(8,128)(2,1)S(1)} fusion(bf16[256,16384]{1,0:T(8,128)(2,1)} %get-tuple-element.8, bf16[16384,1024]{1,0:T(8,128)(2,1)} %param.8), kind=kOutput, calls=%fused_computation.2 | convolution fusion | flops 8590196736 | bytes 42467328 | tf_op jit(solution)/shard_map/dot_general | solution.py:315
  89.0 66.1 %shard_map.74 = bf16[16,16384]{1,0:T(8,128)(2,1)S(1)} custom-call(bf16[256,16384]{1,0:T(8,128)(2,1)} %convolution_convert_fusion.delta, bf16[256,1024]{1,0:T(8,128)(2,1)S(1)} %convolution_convert_fusion.1.base), custom_call_target="tpu_custom_call" | custom-call | tf_op jit(solution)/shard_map/pallas_call | solution.py:267
  155.1 0.8 copy.9
  (3 shorter events, 0.0 us)
Async XLA Ops:
  0.0 0.7 copy-start

commit v5 on v4

--- a/solution.py
+++ b/solution.py
@@ -50,7 +50,8 @@
     rows, width = tok.shape
     part = width // CHUNKS
     right_hops = chips // 2
-    left_hops = chips - 1 - right_hops
+    right_far = [right_hops if k < CHUNKS // 2 else right_hops - 1 for k in range(CHUNKS)]
+    left_far = [chips - 1 - far for far in right_far]
     right, left, sibling = device(position + 1, core), device(position - 1, core), device(position, 1 - core)
     greet_all(n, me)
 
@@ -84,29 +85,23 @@
     own_rows.start()
     own_meta.start()
 
-    def by_right(hop, k):
-        return hop < right_hops or (hop == right_hops and k < CHUNKS // 2)
-
-    def by_left(hop, k):
-        return hop <= left_hops or (hop == right_hops and k >= CHUNKS // 2)
-
     for hop in range(1, right_hops + 1):
         for k in range(CHUNKS):
-            if by_right(hop, k):
+            if hop <= right_far[k]:
                 block = place(device(position - hop, core), k)
                 copy(block, block, right_send.at[hop - 1, k], right_recv.at[hop - 1, k], right).wait_recv()
-                if by_right(hop + 1, k):
+                if hop < right_far[k]:
                     started.append(copy(block, block, right_send.at[hop, k], right_recv.at[hop, k], right))
                     started[-1].start()
                 started.append(copy(block, block, sib_send.at[hop, k], sib_recv.at[hop, k], sibling))
                 started[-1].start()
-            if by_left(hop, k):
+            if hop <= left_far[k]:
                 block = place(device(position + hop, core), k)
                 copy(block, block, left_send.at[hop - 1, k], left_recv.at[hop - 1, k], left).wait_recv()
-                if by_left(hop + 1, k):
+                if hop < left_far[k]:
                     started.append(copy(block, block, left_send.at[hop, k], left_recv.at[hop, k], left))
                     started[-1].start()
-                at = right_hops + hop if hop <= left_hops else hop
+                at = right_hops + hop if hop < right_hops else right_hops
                 started.append(copy(block, block, sib_send.at[at, k], sib_recv.at[at, k], sibling))
                 started[-1].start()
 
@@ -155,13 +150,12 @@
     rows, width = out.shape
     part, piece = width // CHUNKS, width // n
     right_hops = chips // 2
-    left_hops = chips - 1 - right_hops
+    right_far = [right_hops if k < CHUNKS // 2 else right_hops - 1 for k in range(CHUNKS)]
+    left_far = [chips - 1 - far for far in right_far]
     right, left, sibling = device(position + 1, core), device(position - 1, core), device(position, 1 - core)
-    offsets = []
-    for hop in range(right_hops):
-        offsets.append(right_hops - hop)
-        if hop < left_hops:
-            offsets.append(hop - left_hops)
+    offsets = [right_hops]
+    for far in range(right_hops - 1, 0, -1):
+        offsets += [far, -far]
     offsets.append(0)
     greet_all(n, me)
 
@@ -184,7 +178,7 @@
         )
 
     def chip_sum(offset, k):
-        j = offsets.index(offset)
+        j = offsets.index(right_hops if offset == -right_hops else offset)
         sib_copy(j, k).wait_recv()
         return sib[j, :, columns(k)] + delta[block(device(position + offset, core)), columns(k)]
 
@@ -208,12 +202,11 @@
         for k in range(CHUNKS):
             start(sib_copy(j, k))
     for k in range(CHUNKS):
-        j = offsets.index(right_hops)
-        sib[j, :, columns(k)] = chip_sum(right_hops, k)
+        j = offsets.index(right_far[k])
+        sib[j, :, columns(k)] = chip_sum(right_far[k], k)
         to_right(sib.at[j, :, columns(k)], 0, k)
-    for k in range(CHUNKS):
-        j = offsets.index(-left_hops)
-        sib[j, :, columns(k)] = chip_sum(-left_hops, k)
+        j = offsets.index(-left_far[k] if left_far[k] < right_hops else right_hops)
+        sib[j, :, columns(k)] = chip_sum(-left_far[k], k)
         to_left(sib.at[j, :, columns(k)], 0, k)
     for step in range(1, n):
         start(base_copy(step))
@@ -229,12 +222,13 @@
 
     for hop in range(1, right_hops):
         for k in range(CHUNKS):
-            own = chip_sum(right_hops - hop, k)
-            right_arrival(hop - 1, k)
-            from_left[hop - 1, :, columns(k)] = from_left[hop - 1, :, columns(k)] + own
-            to_right(from_left.at[hop - 1, :, columns(k)], hop, k)
-            if hop < left_hops:
-                own = chip_sum(hop - left_hops, k)
+            if hop < right_far[k]:
+                own = chip_sum(right_far[k] - hop, k)
+                right_arrival(hop - 1, k)
+                from_left[hop - 1, :, columns(k)] = from_left[hop - 1, :, columns(k)] + own
+                to_right(from_left.at[hop - 1, :, columns(k)], hop, k)
+            if hop < left_far[k]:
+                own = chip_sum(hop - left_far[k], k)
                 left_arrival(hop - 1, k)
                 from_right[hop - 1, :, columns(k)] = from_right[hop - 1, :, columns(k)] + own
                 to_left(from_right.at[hop - 1, :, columns(k)], hop, k)
@@ -246,9 +240,9 @@
         ).wait_recv()
     for k in range(CHUNKS):
         own = chip_sum(0, k)
-        left_arrival(left_hops - 1, k)
-        right_arrival(right_hops - 1, k)
-        update = own + from_right[left_hops - 1, :, columns(k)] + from_left[right_hops - 1, :, columns(k)]
+        left_arrival(left_far[k] - 1, k)
+        right_arrival(right_far[k] - 1, k)
+        update = own + from_right[left_far[k] - 1, :, columns(k)] + from_left[right_far[k] - 1, :, columns(k)]
         per = n // CHUNKS
         for d in range(per):
             at = k * per + d

time: 156 us -> 153 us (0.981); the launches traced: 156 us -> 150 us
  Pallas kernels: 115 us -> 110 us
    pallas_call x1, Pallas kernels: 66.1 us -> 60.6 us  [reduce_rows(): pl.pallas_call(functools.partial(reduce_kernel, n, snake), out_shape=jax....]
where the time goes in v5:
time: 153 us; the launch traced here: 150 us
  Pallas kernels  110 us (72%)
  matrix products  35.4 us (23%)
  local copies, waits for them, and re-layouts  3.07 us (2%)
  other arithmetic  2.07 us (1%)
    pallas_call x1, Pallas kernels, reduce_rows(): pl.pallas_call(functools.partial(reduce_kernel, n, snake), out_shape=jax....  60.6 us
    pallas_call x1, Pallas kernels, gather(): pl.pallas_call(functools.partial(gather_kernel, n, snake), out_shape=(jax...  49.2 us
    dot_general x1, matrix products, body(): jnp.dot(shrink, expand_blocks.reshape(local_count * rank_size, width), pr...  17.9 us
    dot_general x1, matrix products, body(): jnp.dot(rows, base_weight, preferred_element_type=jnp.float32)  17.4 us

profile of v5, /device:TPU:13, one launch (start us, length us, event | category | flops | bytes accessed | tf_op | source)
XLA Modules:
  0.0 150.4 jit_solution(4255482617708093833)
XLA Ops:
  0.0 0.0 copy-start
  0.0 0.7 fusion.3
  0.7 0.0 copy-done
  0.7 0.6 gather_fusion
  1.3 0.7 and_select_fusion.1
  2.0 0.7 fusion.1
  2.7 0.1 select_n.58
  2.8 0.6 broadcast_in_dim.31.meta
  3.4 49.2 %shard_map.73 = (bf16[256,16384]{1,0:T(8,128)(2,1)}, s32[16,8,128]{2,1,0:T(8,128)}) custom-call(bf16[16,16384]{1,0:T(8,128)(2,1)} %tok.1, s32[8,128]{1,0:T(8,128)} %broadcast_in_dim.31.meta), custom_call_target="tpu_custom_call" | custom-call | tf_op jit(solution)/shard_map/pallas_call | solution.py:127
  52.7 0.9 slice_reduce_fusion
  53.5 0.1 eq.15
  53.6 17.9 %convolution_convert_fusion.delta = bf16[256,16384]{1,0:T(8,128)(2,1)} fusion(bf16[128,16384]{1,0:T(8,128)(2,1)} %bitcast.26, bf16[256,16384]{1,0:T(8,128)(2,1)} %get-tuple-element.8, bf16[128,16384]{1,0:T(8,128)(2,1)} %bitcast.25, s32[128]{0:T(128)S(1)} %fusion.2, s32[256]{0:T(256)S(1)} %eq.15), kind=kOutput, calls=%fused_computation.1 | convolution fusion | flops 2151776256 | bytes 25167360 | tf_op jit(solution)/shard_map/dot_general | solution.py:304
  71.6 17.4 %convolution_convert_fusion.1.base = bf16[256,1024]{1,0:T(8,128)(2,1)S(1)} fusion(bf16[256,16384]{1,0:T(8,128)(2,1)} %get-tuple-element.8, bf16[16384,1024]{1,0:T(8,128)(2,1)} %param.8), kind=kOutput, calls=%fused_computation.2 | convolution fusion | flops 8590196736 | bytes 42467328 | tf_op jit(solution)/shard_map/dot_general | solution.py:309
  89.0 60.6 %shard_map.74 = bf16[16,16384]{1,0:T(8,128)(2,1)S(1)} custom-call(bf16[256,16384]{1,0:T(8,128)(2,1)} %convolution_convert_fusion.delta, bf16[256,1024]{1,0:T(8,128)(2,1)S(1)} %convolution_convert_fusion.1.base), custom_call_target="tpu_custom_call" | custom-call | tf_op jit(solution)/shard_map/pallas_call | solution.py:261
  149.6 0.8 copy.9
  (3 shorter events, 0.0 us)
Async XLA Ops:
  0.0 0.7 copy-start
